TPU v7x, 32 devices: a whole 2x2x4 slice. The times are simulated.
32 devices in a mesh: az: 16 (over z, y, core), mer: 2 (over x).
Axes of the slice: x: 2, y: 2, z: 4, core: 2. Of those that a mesh axis runs over, the one named last changes fastest.
Arguments:
- velocity_modes: bfloat16 [3, 1024, 4096], P(None, 'az', 'mer'), may hold values from -6 to 6
- geometry: float32 [3, 128, 32], P(None, 'az', 'mer'), may hold values from 0.5 to 2
- derivative: float32 [2, 8, 8], replicated, may hold values from -2 to 2
- blade_load: bfloat16 [16, 3, 3, 1024], P('az'), may hold values from -6 to 6
- blade_owner: int32 [36], replicated, may hold values from 0 to 47, as said below
- spread_tile: int32 [2, 16, 4], P('mer', 'az'), may hold values from 0 to 287
- spread_azimuth: bfloat16 [2, 16, 4, 128, 1024], P('mer', 'az'), may hold values from -1.25 to 1.25
- spread_meridional: bfloat16 [2, 16, 4, 128, 128], P('mer', 'az'), may hold values from -1.25 to 1.25
Outputs:
- term_modes: bfloat16 [3, 1024, 4096], P(None, 'az', 'mer')
Inputs may be any that keep to these rules, and one draw needn't show every extreme that they name: Distinct values; blade_owner includes 0 and 47.
All inputs are finite; a program needn't handle non-finite values.
Results may differ from a plain program's by a relative error of at most 0.0073.
Values may be sent and summed in bfloat16 or wider, within the bound.
A program may use at most 64 MiB of HBM per device.

v0:
```python
import functools
import math

import jax
import jax.numpy as jnp
import ml_dtypes
import numpy as np
from jax import lax
from jax.experimental import pallas as pl
from jax.experimental.pallas import tpu as pltpu
from jax.sharding import PartitionSpec as P

PLANES = 1024
TILE = 128


def extended(shard, sides, width):
    for axis, dim in sides:
        count, length = (lax.axis_size(axis), shard.shape[dim])
        up = [(i, (i + 1) % count) for i in range(count - 1)]
        down = [(j, i) for i, j in up]
        last = lax.slice_in_dim(shard, length - width, length, axis=dim)
        leading = lax.slice_in_dim(shard, 0, width, axis=dim)
        before = lax.ppermute(last, axis, up)
        after = lax.ppermute(leading, axis, down)
        shard = jnp.concatenate([before, shard, after], axis=dim)
    return shard


def make_table(planes):
    row_index = jnp.arange(planes, dtype=jnp.int32)
    wave_index = row_index // 2
    phase_index = row_index[:, None] * wave_index[None, :] % planes
    angle_rad = phase_index.astype(jnp.float32) * (2.0 * math.pi / planes)
    even_rows = (row_index % 2 == 0)[None, :]
    dft_table = math.sqrt(2.0 / planes) * jnp.where(
        even_rows, jnp.cos(angle_rad), -jnp.sin(angle_rad)
    )
    return dft_table.astype(jnp.bfloat16)


def slope_of(mode_block, first_pair, planes):
    shape_all = mode_block.shape
    mode_pairs = mode_block.reshape(shape_all[0], shape_all[1] // 2, 2, shape_all[2]).astype(
        jnp.float32
    )
    wave_number = (first_pair + jnp.arange(shape_all[1] // 2, dtype=jnp.int32)).astype(
        jnp.float32
    ) * (2.0 * math.pi / planes)
    wave_number = wave_number[None, :, None]
    result = jnp.stack(
        [-wave_number * mode_pairs[:, :, 1], wave_number * mode_pairs[:, :, 0]], axis=2
    )
    return result.reshape(shape_all).astype(jnp.bfloat16)


def inverse_of(dft_table, mode_block):
    return jnp.einsum("pj,cjn->cpn", dft_table, mode_block, preferred_element_type=jnp.float32)


def slopes_of(velocity, geometry, derivative):
    hp = lax.Precision.HIGHEST
    shape_all = velocity.shape
    elem_size = derivative.shape[1]
    elements = shape_all[3] // elem_size
    radial_slope = geometry[1] * jnp.einsum("rs,cpsz->cprz", derivative[0], velocity, precision=hp)
    blocks = velocity.reshape(shape_all[0], shape_all[1], shape_all[2], elements, elem_size)
    raw_slope = jnp.einsum("at,cpret->cprea", derivative[1], blocks, precision=hp)
    axial_slope = raw_slope * geometry[2].reshape(shape_all[2], elements, elem_size)
    first_face = axial_slope[..., 0]
    last_face = axial_slope[..., elem_size - 1]
    face_mean = 0.5 * (last_face[..., :-1] + first_face[..., 1:])
    new_first = first_face.at[..., 1:].set(face_mean)
    new_last = last_face.at[..., :-1].set(face_mean)
    return (radial_slope, axial_slope, first_face, last_face, new_first, new_last)


def advect(velocity, radial_slope, axial_slope, swirl_slope, inverse_radius):
    radial_vel = velocity[0]
    swirl_vel = velocity[1]
    axial_vel = velocity[2]
    advection = (
        radial_vel[None] * radial_slope
        + axial_vel[None] * axial_slope
        + (inverse_radius * swirl_vel)[None] * swirl_slope
    )
    advection = advection.at[0].add(-(inverse_radius * swirl_vel * swirl_vel))
    advection = advection.at[1].add(inverse_radius * radial_vel * swirl_vel)
    return advection


def forcing_of(all_loads, tile_ids, spread_az, spread_mer, tile_size):
    blades = all_loads.shape[0]
    tiles_count = all_loads.shape[2] // tile_size
    tile_loads = (
        all_loads.reshape(blades, 3, tiles_count, tile_size)
        .transpose(0, 2, 1, 3)
        .reshape(blades * tiles_count, 3, tile_size)
    )
    picked = jnp.take(tile_loads, tile_ids, axis=0)
    scaled = (
        picked.astype(jnp.float32)[:, :, :, None] * spread_mer.astype(jnp.float32)[:, None, :, :]
    ).astype(jnp.bfloat16)
    return jnp.einsum("jmp,jcmn->cpn", spread_az, scaled, preferred_element_type=jnp.float32)


def on_device(
    velocity_modes,
    geometry,
    derivative,
    blade_load,
    blade_owner,
    spread_tile,
    spread_azimuth,
    spread_meridional,
):
    planes = PLANES
    dft_table = make_table(planes)
    local_modes = velocity_modes.shape[1]
    block_cells = geometry.shape[1] * geometry.shape[2]
    first_pair = lax.axis_index("az") * (local_modes // 2)
    slope_local = slope_of(velocity_modes, first_pair, planes)
    velocity = inverse_of(
        dft_table, lax.all_to_all(velocity_modes, "az", split_axis=2, concat_axis=1, tiled=True)
    )
    swirl_slope = inverse_of(
        dft_table, lax.all_to_all(slope_local, "az", split_axis=2, concat_axis=1, tiled=True)
    )
    rows = geometry.shape[1]
    cells = geometry.shape[2]
    velocity = velocity.reshape(3, planes, rows, cells)
    swirl_slope = swirl_slope.reshape(3, planes, rows, cells)
    radial_slope, axial_slope, first_face, last_face, new_first, new_last = slopes_of(
        velocity, geometry, derivative
    )
    edge_values = jnp.stack([first_face[..., 0], last_face[..., -1]], axis=-1)
    padded = extended(edge_values.astype(jnp.bfloat16), (("mer", 3),), 1).astype(edge_values.dtype)
    mer_index = lax.axis_index("mer")
    mer_count = lax.axis_size("mer")
    left_value = jnp.where(
        mer_index > 0, 0.5 * (padded[..., 0] + first_face[..., 0]), first_face[..., 0]
    )
    right_value = jnp.where(
        mer_index < mer_count - 1, 0.5 * (last_face[..., -1] + padded[..., 3]), last_face[..., -1]
    )
    new_first = new_first.at[..., 0].set(left_value)
    new_last = new_last.at[..., -1].set(right_value)
    elem_size = derivative.shape[1]
    axial_slope = axial_slope.at[..., 0].set(new_first).at[..., elem_size - 1].set(new_last)
    axial_slope = axial_slope.reshape(3, planes, rows, cells)
    advection = advect(velocity, radial_slope, axial_slope, swirl_slope, geometry[0])
    local_slots = blade_load[0]
    every_slot = lax.all_gather(blade_load, "az", axis=0, tiled=True)
    all_loads = every_slot.reshape(-1, 3, local_slots.shape[2])[blade_owner]
    forcing = forcing_of(
        all_loads, spread_tile[0, 0], spread_azimuth[0, 0], spread_meridional[0, 0], TILE
    )
    total_term = (advection.reshape(3, planes, block_cells) + forcing).astype(jnp.bfloat16)
    result = jnp.einsum(
        "pj,cpn->cjn", dft_table, total_term, preferred_element_type=jnp.float32
    ).astype(jnp.bfloat16)
    return lax.all_to_all(result, "az", split_axis=1, concat_axis=2, tiled=True)


CHUNK = 256
MESH = pl.DeviceIdType.MESH
HP = lax.Precision.HIGHEST
NT = (((1,), (1,)), ((), ()))
TN = (((0,), (0,)), ((), ()))


def host_table(planes):
    row_index = np.arange(planes, dtype=np.int32)
    phase = (row_index[:, None] * (row_index // 2)[None, :]) % planes
    angle = phase.astype(np.float32) * np.float32(2.0 * math.pi / planes)
    even = (row_index % 2 == 0)[None, :]
    table = np.float32(math.sqrt(2.0 / planes)) * np.where(even, np.cos(angle), -np.sin(angle))
    return table.astype(np.float32).astype(ml_dtypes.bfloat16)


def iota(shape, dim):
    return lax.broadcasted_iota(jnp.int32, shape, dim)


def dot_f32(a, b, dims):
    return lax.dot_general(a, b, dims, precision=HP, preferred_element_type=jnp.float32)


def dot_bf16(a, b, dims=(((1,), (0,)), ((), ()))):
    return lax.dot_general(a, b, dims, preferred_element_type=jnp.float32)


def geometry_row(geo, cells, nodes):
    rows = geo.shape[0]
    spread = (iota((cells, nodes), 1) % cells == iota((cells, nodes), 0)).astype(jnp.float32)
    wide = dot_f32(geo, spread, (((1,), (0,)), ((), ())))
    own = iota((rows, nodes), 1) // cells == iota((rows, nodes), 0)
    return jnp.sum(jnp.where(own, wide, 0.0), axis=0, keepdims=True)


def slope_matrices(der, metric_r, metric_z, rows, cells, edge):
    elem = der.shape[1]
    nodes = rows * cells
    left, right = iota((nodes, nodes), 0), iota((nodes, nodes), 1)
    by_row = (iota((nodes, elem), 0) // cells == iota((nodes, elem), 1)).astype(jnp.float32)
    by_axial = (iota((nodes, elem), 0) % elem == iota((nodes, elem), 1)).astype(jnp.float32)
    radial = dot_f32(dot_f32(by_row, der[0], NT), by_row, NT)
    radial = jnp.where(left % cells == right % cells, radial, 0.0) * metric_r
    axial = dot_f32(dot_f32(by_axial, der[1], NT), by_axial, NT)
    axial = jnp.where(left // elem == right // elem, axial, 0.0) * metric_z
    following = pltpu.roll(axial, nodes - 1, 1)
    previous = pltpu.roll(axial, 1, 1)
    cell = right % cells
    last = (cell % elem == elem - 1) & (cell != cells - 1)
    first = (cell % elem == 0) & (cell != 0)
    mean = jnp.where(last, 0.5 * (axial + following), axial)
    mean = jnp.where(first, 0.5 * (axial + previous), mean)
    mean = jnp.where(cell == edge, 0.5 * axial, mean)
    return radial, mean


def fused_kernel(
    n,
    slots,
    vm,
    geo,
    der,
    loads,
    owner,
    tile,
    sa,
    sm,
    table,
    table_t,
    out,
    recv,
    rhs,
    vel,
    swirl,
    radial,
    axial,
    forcing,
    total,
    res,
    tab_v,
    tabt_v,
    sa_v,
    scaled,
    gmat,
    load_rows,
    ids_send,
    ids_recv,
    pick_send,
    pick_recv,
    face_send,
    face_recv,
    f_send,
    f_recv,
    b_send,
    b_recv,
    small_send,
    small_recv,
    x_send,
    x_recv,
    local_sem,
):
    me = lax.axis_index("az")
    mer = lax.axis_index("mer")
    local = vm.shape[1]
    planes = table.shape[0]
    rows, cells = geo.shape[1], geo.shape[2]
    nodes = rows * cells
    jobs = sm.shape[2]
    steps = planes // CHUNK
    bf16 = jnp.bfloat16

    loading = [
        pltpu.make_async_copy(table, tab_v, local_sem.at[0]),
        pltpu.make_async_copy(table_t, tabt_v, local_sem.at[1]),
        pltpu.make_async_copy(sa.at[0, 0], sa_v, local_sem.at[2]),
    ]

    barrier = pltpu.get_barrier_semaphore()

    def greet(o, carry):
        pl.semaphore_signal(
            barrier, inc=1, device_id=(lax.rem(me + o, n), mer), device_id_type=MESH
        )
        return carry

    lax.fori_loop(1, n, greet, 0)
    pl.semaphore_signal(barrier, inc=1, device_id=(me, 1 - mer), device_id_type=MESH)

    row8 = iota((8, 128), 0) % jobs
    codes = jnp.zeros((8, 128), jnp.int32)
    tiles_per_blade = loads.shape[3] // 128
    for j in range(jobs):
        t = tile[0, 0, j]
        code = owner[t // tiles_per_blade] * tiles_per_blade + lax.rem(t, tiles_per_blade)
        codes = jnp.where(row8 == j, code, codes)
    ids_send[...] = codes
    ids_recv[pl.ds(pl.multiple_of(me * 8, 8), 8), :] = codes

    pl.semaphore_wait(barrier, n)

    def send_ids(o, carry):
        peer = lax.rem(me + o, n)
        pltpu.make_async_remote_copy(
            src_ref=ids_send,
            dst_ref=ids_recv.at[pl.ds(pl.multiple_of(me * 8, 8), 8), :],
            send_sem=small_send.at[0],
            recv_sem=small_recv.at[0],
            device_id=(peer, mer),
            device_id_type=MESH,
        ).start()
        return carry

    lax.fori_loop(1, n, send_ids, 0)

    def send_forward(c):
        def body(o, carry):
            peer = lax.rem(me + o, n)
            pltpu.make_async_remote_copy(
                src_ref=vm.at[c, :, pl.ds(pl.multiple_of(peer * nodes, nodes), nodes)],
                dst_ref=recv.at[c, pl.ds(pl.multiple_of(me * local, local), local), :],
                send_sem=f_send.at[c],
                recv_sem=f_recv.at[c],
                device_id=(peer, mer),
                device_id_type=MESH,
            ).start()
            return carry

        lax.fori_loop(1, n, body, 0)
        pltpu.make_async_copy(
            vm.at[c, :, pl.ds(pl.multiple_of(me * nodes, nodes), nodes)],
            recv.at[c, pl.ds(pl.multiple_of(me * local, local), local), :],
            f_recv.at[c],
        ).start()

    send_forward(0)
    send_forward(1)
    for copy in loading:
        copy.start()

    load_rows[...] = jnp.zeros(load_rows.shape, jnp.float32)
    for s in range(slots):
        load_rows[3 * s : 3 * s + 3, :] = loads[0, s].astype(jnp.float32)

    pltpu.make_async_copy(
        ids_recv.at[pl.ds(0, (n - 1) * 8), :],
        ids_recv.at[pl.ds(0, (n - 1) * 8), :],
        small_recv.at[0],
    ).wait()
    asked = ids_recv[...].reshape(n, 8, 128)
    asked = jnp.concatenate([asked, asked], axis=1).reshape(n * 16, 128)
    part = (iota((n * 16, 128), 0) % 16) // jobs
    slot = asked // tiles_per_blade - me * slots
    wanted = slot * 3 + part
    held = (slot >= 0) & (slot < slots) & (part < 3)
    chosen = jnp.where(held & (iota((n * 16, 128), 1) == wanted), 1.0, 0.0)
    every = dot_bf16(chosen[:, :16].astype(bf16), load_rows[...].astype(bf16))
    tile_of = lax.rem(asked, tiles_per_blade)
    picks = jnp.zeros((n * 16, 128), jnp.float32)
    for t in range(tiles_per_blade):
        picks = picks + jnp.where(tile_of == t, every[:, t * 128 : (t + 1) * 128], 0.0)
    pick_send[...] = picks.astype(bf16)
    pick_recv[pl.ds(pl.multiple_of(me * 16, 16), 16), :] = pick_send[
        pl.ds(pl.multiple_of(me * 16, 16), 16), :
    ]

    def send_picks(o, carry):
        peer = lax.rem(me + o, n)
        pltpu.make_async_remote_copy(
            src_ref=pick_send.at[pl.ds(pl.multiple_of(peer * 16, 16), 16), :],
            dst_ref=pick_recv.at[pl.ds(pl.multiple_of(me * 16, 16), 16), :],
            send_sem=small_send.at[1],
            recv_sem=small_recv.at[1],
            device_id=(peer, mer),
            device_id_type=MESH,
        ).start()
        return carry

    lax.fori_loop(1, n, send_picks, 0)
    send_forward(2)

    edge = (1 - mer) * (cells - 1)
    q = geometry_row(geo[0], cells, nodes)
    grad_r, grad_z = slope_matrices(
        der,
        geometry_row(geo[1], cells, nodes),
        geometry_row(geo[2], cells, nodes),
        rows,
        cells,
        edge,
    )
    for side, grad in ((0, grad_r), (1, grad_z)):
        high = grad.astype(bf16)
        low = (grad - high.astype(jnp.float32)).astype(bf16)
        at = slice(side * nodes, (side + 1) * nodes)
        gmat[0:nodes, at] = high
        gmat[nodes : 2 * nodes, at] = high
        gmat[2 * nodes : 3 * nodes, at] = low
    lane = iota((rows, nodes), 1)
    on_edge = (lane // cells == iota((rows, nodes), 0)) & (lane % cells == edge)
    take_edge = jnp.where(on_edge, 2.0, 0.0).astype(bf16)
    put_edge = jnp.where(on_edge, 0.5, 0.0).astype(bf16)

    loading[0].wait()

    def to_planes(c):
        pltpu.make_async_copy(recv.at[c], recv.at[c], f_recv.at[c]).wait()
        modes = recv[c]
        wide = modes.astype(jnp.float32)
        index = iota((planes, nodes), 0)
        wave = (index // 2).astype(jnp.float32) * (2.0 * math.pi / planes)
        after = pltpu.roll(wide, planes - 1, 0)
        before = pltpu.roll(wide, 1, 0)
        slope = jnp.where(index % 2 == 0, -wave * after, wave * before)
        rhs[:, 0:nodes] = modes
        rhs[:, nodes : 2 * nodes] = slope.astype(bf16)

        def body(s, carry):
            at = pl.ds(pl.multiple_of(s * CHUNK, CHUNK), CHUNK)
            both = dot_bf16(tab_v[at, :], rhs[...])
            u = both[:, 0:nodes]
            vel[c, at, :] = u
            swirl[c, at, :] = both[:, nodes : 2 * nodes]
            high = u.astype(bf16)
            low = (u - high.astype(jnp.float32)).astype(bf16)
            slopes = dot_bf16(jnp.concatenate([high, low, high], axis=1), gmat[...])
            radial[c, at, :] = slopes[:, 0:nodes]
            sz = slopes[:, nodes : 2 * nodes]
            axial[c, at, :] = sz
            face_send[c, :, at] = dot_bf16(take_edge, sz.astype(bf16), NT)
            return carry

        lax.fori_loop(0, steps, body, 0)
        copy = pltpu.make_async_remote_copy(
            src_ref=face_send.at[c],
            dst_ref=face_recv.at[c],
            send_sem=x_send.at[c],
            recv_sem=x_recv.at[c],
            device_id=(me, 1 - mer),
            device_id_type=MESH,
        )
        copy.start()
        return copy

    faces = [to_planes(0)]

    pltpu.make_async_copy(
        pick_recv.at[pl.ds(0, (n - 1) * 16), :],
        pick_recv.at[pl.ds(0, (n - 1) * 16), :],
        small_recv.at[1],
    ).wait()
    picked = jnp.sum(pick_recv[...].astype(jnp.float32).reshape(n, 16, 128), axis=0).astype(bf16)
    unit = (iota((128, 128), 0) == iota((128, 128), 1)).astype(jnp.float32).astype(bf16)
    columns = dot_bf16(unit, picked, NT)
    for j in range(jobs):
        weight = sm[0, 0, j].astype(jnp.float32)
        for i in range(3):
            column = columns[:, i * jobs + j : i * jobs + j + 1]
            scaled[j * 128 : (j + 1) * 128, i * nodes : (i + 1) * nodes] = (
                column * weight
            ).astype(bf16)
    loading[2].wait()

    def force(s, carry):
        at = pl.ds(pl.multiple_of(s * CHUNK, CHUNK), CHUNK)
        lhs = sa_v[:, :, at].reshape(jobs * 128, CHUNK)
        forcing[at, :] = dot_bf16(lhs, scaled[...], TN)
        return carry

    lax.fori_loop(0, steps, force, 0)

    faces.append(to_planes(1))
    faces.append(to_planes(2))
    loading[1].wait()

    def to_modes(i):
        faces[i].wait()

        def term(s, carry):
            at = pl.ds(pl.multiple_of(s * CHUNK, CHUNK), CHUNK)
            ur, ut, uz = vel[0, at, :], vel[1, at, :], vel[2, at, :]
            other = dot_bf16(face_recv[i, :, at].astype(bf16), put_edge, TN)
            slope_z = axial[i, at, :] + other
            qt = q * ut
            value = ur * radial[i, at, :] + uz * slope_z + qt * swirl[i, at, :]
            if i == 0:
                value = value - qt * ut
            if i == 1:
                value = value + qt * ur
            total[at, :] = (value + forcing[at, i * nodes : (i + 1) * nodes]).astype(bf16)
            return carry

        lax.fori_loop(0, steps, term, 0)

        def back(s, carry):
            at = pl.ds(pl.multiple_of(s * CHUNK, CHUNK), CHUNK)
            res[i, at, :] = dot_bf16(tabt_v[at, :], total[...]).astype(bf16)
            return carry

        lax.fori_loop(0, steps, back, 0)

        def send(o, carry):
            peer = lax.rem(me + o, n)
            pltpu.make_async_remote_copy(
                src_ref=res.at[i, pl.ds(pl.multiple_of(peer * local, local), local), :],
                dst_ref=out.at[i, :, pl.ds(pl.multiple_of(me * nodes, nodes), nodes)],
                send_sem=b_send.at[i],
                recv_sem=b_recv.at[i],
                device_id=(peer, mer),
                device_id_type=MESH,
            ).start()
            return carry

        lax.fori_loop(1, n, send, 0)
        pltpu.make_async_copy(
            res.at[i, pl.ds(pl.multiple_of(me * local, local), local), :],
            out.at[i, :, pl.ds(pl.multiple_of(me * nodes, nodes), nodes)],
            b_recv.at[i],
        ).start()

    for i in range(3):
        to_modes(i)

    sent = recv.at[0, pl.ds(0, (n - 1) * local), :]
    for c in range(3):
        pltpu.make_async_copy(sent, sent, f_send.at[c]).wait()
        pltpu.make_async_copy(sent, sent, b_send.at[c]).wait()
    sent = ids_recv.at[pl.ds(0, (n - 1) * 8), :]
    pltpu.make_async_copy(sent, sent, small_send.at[0]).wait()
    sent = pick_recv.at[pl.ds(0, (n - 1) * 16), :]
    pltpu.make_async_copy(sent, sent, small_send.at[1]).wait()
    for c in range(3):
        pltpu.make_async_copy(out.at[c], out.at[c], b_recv.at[c]).wait()


def on_device_fused(
    velocity_modes,
    geometry,
    derivative,
    blade_load,
    blade_owner,
    spread_tile,
    spread_azimuth,
    spread_meridional,
):
    n = lax.axis_size("az")
    local = velocity_modes.shape[1]
    planes = n * local
    rows, cells = geometry.shape[1], geometry.shape[2]
    nodes = rows * cells
    jobs = spread_tile.shape[2]
    slots = blade_load.shape[1]
    if local % 16 or lax.axis_size("mer") != 2 or 3 * slots > 16 or jobs != 4:
        return on_device(
            velocity_modes,
            geometry,
            derivative,
            blade_load,
            blade_owner,
            spread_tile,
            spread_azimuth,
            spread_meridional,
        )
    table = host_table(planes)
    bf16, f32 = jnp.bfloat16, jnp.float32
    vmem = pl.BlockSpec(memory_space=pltpu.VMEM)
    smem = pl.BlockSpec(memory_space=pltpu.SMEM)
    hbm = pl.BlockSpec(memory_space=pl.ANY)
    dma = pltpu.SemaphoreType.DMA
    return pl.pallas_call(
        functools.partial(fused_kernel, n, slots),
        out_shape=jax.ShapeDtypeStruct(velocity_modes.shape, bf16),
        in_specs=[hbm, vmem, vmem, vmem, smem, smem, hbm, vmem, hbm, hbm],
        out_specs=hbm,
        scratch_shapes=[
            pltpu.VMEM((3, planes, nodes), bf16),
            pltpu.VMEM((planes, 2 * nodes), bf16),
            pltpu.VMEM((3, planes, nodes), f32),
            pltpu.VMEM((3, planes, nodes), f32),
            pltpu.VMEM((3, planes, nodes), f32),
            pltpu.VMEM((3, planes, nodes), f32),
            pltpu.VMEM((planes, 3 * nodes), f32),
            pltpu.VMEM((planes, nodes), bf16),
            pltpu.VMEM((3, planes, nodes), bf16),
            pltpu.VMEM((planes, planes), bf16),
            pltpu.VMEM((planes, planes), bf16),
            pltpu.VMEM((jobs, TILE, planes), bf16),
            pltpu.VMEM((jobs * TILE, 3 * nodes), bf16),
            pltpu.VMEM((3 * nodes, 2 * nodes), bf16),
            pltpu.VMEM((16, blade_load.shape[3]), f32),
            pltpu.VMEM((8, 128), jnp.int32),
            pltpu.VMEM((n * 8, 128), jnp.int32),
            pltpu.VMEM((n * 16, 128), bf16),
            pltpu.VMEM((n * 16, 128), bf16),
            pltpu.VMEM((3, rows, planes), f32),
            pltpu.VMEM((3, rows, planes), f32),
            dma((3,)),
            dma((3,)),
            dma((3,)),
            dma((3,)),
            dma((2,)),
            dma((2,)),
            dma((3,)),
            dma((3,)),
            dma((3,)),
        ],
        compiler_params=pltpu.CompilerParams(
            collective_id=0, has_side_effects=True, vmem_limit_bytes=48 * 1024 * 1024
        ),
    )(
        velocity_modes,
        geometry,
        derivative,
        blade_load,
        blade_owner,
        spread_tile,
        spread_azimuth,
        spread_meridional,
        jnp.asarray(table),
        jnp.asarray(np.ascontiguousarray(table.T)),
    )


def solution(mesh):
    in_specs = (
        P(None, "az", "mer"),
        P(None, "az", "mer"),
        P(),
        P("az", None, None, None),
        P(),
        P("mer", "az", None),
        P("mer", "az", None, None, None),
        P("mer", "az", None, None, None),
    )
    out_specs = P(None, "az", "mer")
    return jax.shard_map(
        on_device_fused, mesh=mesh, in_specs=in_specs, out_specs=out_specs, check_vma=False
    )
```

profile of v0, /device:TPU:0, one launch (start us, length us, event | category | flops | bytes accessed | tf_op | source)
XLA Modules:
  0.0 62.5 jit_solution(8521521132081497825)
XLA Ops:
  0.0 0.0 copy-start
  0.0 1.6 %copy-done = bf16[1024,1024]{1,0:T(8,128)(2,1)S(1)} copy-done((bf16[1024,1024]{1,0:T(8,128)(2,1)S(1)}, bf16[1024,1024]{1,0:T(8,128)(2,1)}, u32[]{:S(2)}) %copy-start) | copy-done | bytes 2097176
  1.6 0.0 copy-start.1
  1.6 1.2 %copy-done.1 = bf16[1,1,4,128,1024]{4,3,2,1,0:T(8,128)(2,1)S(1)} copy-done((bf16[1,1,4,128,1024]{4,3,2,1,0:T(8,128)(2,1)S(1)}, bf16[1,1,4,128,1024]{4,3,2,1,0:T(8,128)(2,1)}, u32[]{:S(2)}) %copy-start.1) | copy-done | bytes 1048600
  2.8 0.0 copy-start.2
  2.8 1.1 %copy-done.2 = bf16[3,64,2048]{2,1,0:T(8,128)(2,1)S(1)} copy-done((bf16[3,64,2048]{2,1,0:T(8,128)(2,1)S(1)}, bf16[3,64,2048]{2,1,0:T(8,128)(2,1)}, u32[]{:S(2)}) %copy-start.2) | copy-done | bytes 786456
  4.0 0.0 copy-start.3
  4.0 0.9 %copy-done.3 = bf16[1,1,4,128,128]{4,3,2,1,0:T(8,128)(2,1)S(1)} copy-done((bf16[1,1,4,128,128]{4,3,2,1,0:T(8,128)(2,1)S(1)}, bf16[1,1,4,128,128]{4,3,2,1,0:T(8,128)(2,1)}, u32[]{:S(2)}) %copy-start.3) | copy-done | bytes 131096
  4.9 0.0 copy-start.4
  4.9 0.7 %copy-done.4 = bf16[1,3,3,1024]{3,2,1,0:T(4,128)(2,1)S(1)} copy-done((bf16[1,3,3,1024]{3,2,1,0:T(4,128)(2,1)S(1)}, bf16[1,3,3,1024]{3,2,1,0:T(4,128)(2,1)}, u32[]{:S(2)}) %copy-start.4) | copy-done | bytes 18456
  5.6 0.0 copy-start.5
  5.6 0.7 %copy-done.5 = f32[3,8,16]{2,1,0:T(8,128)S(1)} copy-done((f32[3,8,16]{2,1,0:T(8,128)S(1)}, f32[3,8,16]{2,1,0:T(8,128)}, u32[]{:S(2)}) %copy-start.5) | copy-done | bytes 1560
  6.3 0.0 copy-start.6
  6.3 0.7 %copy-done.6 = f32[2,8,8]{2,1,0:T(8,128)S(1)} copy-done((f32[2,8,8]{2,1,0:T(8,128)S(1)}, f32[2,8,8]{2,1,0:T(8,128)}, u32[]{:S(2)}) %copy-start.6) | copy-done | bytes 536
  7.0 0.0 copy-start.7
  7.0 0.7 %copy-done.7 = s32[36]{0:T(128)S(1)} copy-done((s32[36]{0:T(128)S(1)}, s32[36]{0:T(128)}, u32[]{:S(2)}) %copy-start.7) | copy-done | bytes 168
  7.7 0.0 copy-start.8
  7.7 0.7 %copy-done.8 = s32[1,1,4]{2,1,0:T(1,128)S(1)} copy-done((s32[1,1,4]{2,1,0:T(1,128)S(1)}, s32[1,1,4]{2,1,0:T(1,128)}, u32[]{:S(2)}) %copy-start.8) | copy-done | bytes 40
  8.3 53.3 %shard_map.100 = bf16[3,64,2048]{2,1,0:T(8,128)(2,1)S(1)} custom-call(bf16[3,64,2048]{2,1,0:T(8,128)(2,1)S(1)} %copy-done.2, f32[3,8,16]{2,1,0:T(8,128)S(1)} %copy-done.5, f32[2,8,8]{2,1,0:T(8,128)S(1)} %copy-done.6, bf16[1,3,3,1024]{3,2,1,0:T(4,128)(2,1)S(1)} %copy-done.4, s32[36]{0:T(128)S(1)} %copy-done.7, s32[1,1,4]{2,1,0:T(1,128)S(1)} %copy-done.8, ...), custom_call_target="tpu_custom_call" | custom-call | tf_op jit(solution)/shard_map/pallas_call | solution.py:574
  61.6 0.9 %copy.12 = bf16[3,64,2048]{2,1,0:T(8,128)(2,1)} copy(bf16[3,64,2048]{2,1,0:T(8,128)(2,1)S(1)} %shard_map.100) | data formatting | bytes 1572864
Async XLA Ops:
  0.0 1.6 %copy-start = (bf16[1024,1024]{1,0:T(8,128)(2,1)S(1)}, bf16[1024,1024]{1,0:T(8,128)(2,1)}, u32[]{:S(2)}) copy-start(bf16[1024,1024]{1,0:T(8,128)(2,1)} %constant.4.clone.table) | copy-start | bytes 6291460
  1.6 1.2 %copy-start.1 = (bf16[1,1,4,128,1024]{4,3,2,1,0:T(8,128)(2,1)S(1)}, bf16[1,1,4,128,1024]{4,3,2,1,0:T(8,128)(2,1)}, u32[]{:S(2)}) copy-start(bf16[1,1,4,128,1024]{4,3,2,1,0:T(8,128)(2,1)} %sa.1) | copy-start | bytes 3145732
  2.8 1.1 %copy-start.2 = (bf16[3,64,2048]{2,1,0:T(8,128)(2,1)S(1)}, bf16[3,64,2048]{2,1,0:T(8,128)(2,1)}, u32[]{:S(2)}) copy-start(bf16[3,64,2048]{2,1,0:T(8,128)(2,1)} %vm.1) | copy-start | bytes 2359300
  4.0 0.9 %copy-start.3 = (bf16[1,1,4,128,128]{4,3,2,1,0:T(8,128)(2,1)S(1)}, bf16[1,1,4,128,128]{4,3,2,1,0:T(8,128)(2,1)}, u32[]{:S(2)}) copy-start(bf16[1,1,4,128,128]{4,3,2,1,0:T(8,128)(2,1)} %sm.1) | copy-start | bytes 393220
  4.9 0.7 %copy-start.4 = (bf16[1,3,3,1024]{3,2,1,0:T(4,128)(2,1)S(1)}, bf16[1,3,3,1024]{3,2,1,0:T(4,128)(2,1)}, u32[]{:S(2)}) copy-start(bf16[1,3,3,1024]{3,2,1,0:T(4,128)(2,1)} %loads.1) | copy-start | bytes 55300
  5.6 0.7 %copy-start.5 = (f32[3,8,16]{2,1,0:T(8,128)S(1)}, f32[3,8,16]{2,1,0:T(8,128)}, u32[]{:S(2)}) copy-start(f32[3,8,16]{2,1,0:T(8,128)} %geo.1) | copy-start | bytes 4612
  6.3 0.7 %copy-start.6 = (f32[2,8,8]{2,1,0:T(8,128)S(1)}, f32[2,8,8]{2,1,0:T(8,128)}, u32[]{:S(2)}) copy-start(f32[2,8,8]{2,1,0:T(8,128)} %der.1) | copy-start | bytes 1540
  7.0 0.7 %copy-start.7 = (s32[36]{0:T(128)S(1)}, s32[36]{0:T(128)}, u32[]{:S(2)}) copy-start(s32[36]{0:T(128)} %owner.1) | copy-start | bytes 436
  7.7 0.7 %copy-start.8 = (s32[1,1,4]{2,1,0:T(1,128)S(1)}, s32[1,1,4]{2,1,0:T(1,128)}, u32[]{:S(2)}) copy-start(s32[1,1,4]{2,1,0:T(1,128)} %tile.1) | copy-start | bytes 52
where the time goes:
time: 62.9 us; the launch traced here: 62.5 us
  Pallas kernels  53.3 us (85%)
  local copies, waits for them, and re-layouts  9.18 us (15%)
    pallas_call x1, Pallas kernels, on_device_fused(): pl.pallas_call(functools.partial(fused_kernel, n, slots), out_shape=jax.S...  53.3 us
    unnamed x19, local copies, waits for them, and re-layouts  9.18 us

commit v1 on v0

--- a/solution.py
+++ b/solution.py
@@ -223,13 +223,13 @@
     n,
     slots,
     vm,
-    geo,
-    der,
+    geo_in,
+    der_in,
     loads,
     owner,
     tile,
     sa,
-    sm,
+    sm_in,
     table,
     table_t,
     out,
@@ -245,6 +245,9 @@
     tab_v,
     tabt_v,
     sa_v,
+    sm,
+    geo,
+    der,
     scaled,
     gmat,
     load_rows,
@@ -270,15 +273,9 @@
     planes = table.shape[0]
     rows, cells = geo.shape[1], geo.shape[2]
     nodes = rows * cells
-    jobs = sm.shape[2]
+    jobs = sm.shape[0]
     steps = planes // CHUNK
     bf16 = jnp.bfloat16
-
-    loading = [
-        pltpu.make_async_copy(table, tab_v, local_sem.at[0]),
-        pltpu.make_async_copy(table_t, tabt_v, local_sem.at[1]),
-        pltpu.make_async_copy(sa.at[0, 0], sa_v, local_sem.at[2]),
-    ]
 
     barrier = pltpu.get_barrier_semaphore()
 
@@ -290,6 +287,15 @@
 
     lax.fori_loop(1, n, greet, 0)
     pl.semaphore_signal(barrier, inc=1, device_id=(me, 1 - mer), device_id_type=MESH)
+
+    loading = [
+        pltpu.make_async_copy(geo_in, geo, local_sem.at[0]),
+        pltpu.make_async_copy(der_in, der, local_sem.at[1]),
+        pltpu.make_async_copy(sm_in.at[0, 0], sm, local_sem.at[2]),
+        pltpu.make_async_copy(sa.at[0, 0], sa_v, local_sem.at[3]),
+        pltpu.make_async_copy(table, tab_v, local_sem.at[4]),
+        pltpu.make_async_copy(table_t, tabt_v, local_sem.at[5]),
+    ]
 
     row8 = iota((8, 128), 0) % jobs
     codes = jnp.zeros((8, 128), jnp.int32)
@@ -338,7 +344,6 @@
         ).start()
 
     send_forward(0)
-    send_forward(1)
     for copy in loading:
         copy.start()
 
@@ -381,8 +386,11 @@
         return carry
 
     lax.fori_loop(1, n, send_picks, 0)
+    send_forward(1)
     send_forward(2)
 
+    loading[0].wait()
+    loading[1].wait()
     edge = (1 - mer) * (cells - 1)
     q = geometry_row(geo[0], cells, nodes)
     grad_r, grad_z = slope_matrices(
@@ -405,37 +413,37 @@
     take_edge = jnp.where(on_edge, 2.0, 0.0).astype(bf16)
     put_edge = jnp.where(on_edge, 0.5, 0.0).astype(bf16)
 
-    loading[0].wait()
-
-    def to_planes(c):
+    def over_planes(body, unroll=False):
+        def step(s, carry):
+            body(pl.ds(pl.multiple_of(s * CHUNK, CHUNK), CHUNK))
+            return carry
+
+        lax.fori_loop(0, steps, step, 0, unroll=unroll)
+
+    def arrived(c):
         pltpu.make_async_copy(recv.at[c], recv.at[c], f_recv.at[c]).wait()
-        modes = recv[c]
-        wide = modes.astype(jnp.float32)
+
+    def slope_modes(c):
+        wide = recv[c].astype(jnp.float32)
         index = iota((planes, nodes), 0)
         wave = (index // 2).astype(jnp.float32) * (2.0 * math.pi / planes)
         after = pltpu.roll(wide, planes - 1, 0)
         before = pltpu.roll(wide, 1, 0)
-        slope = jnp.where(index % 2 == 0, -wave * after, wave * before)
-        rhs[:, 0:nodes] = modes
-        rhs[:, nodes : 2 * nodes] = slope.astype(bf16)
-
-        def body(s, carry):
-            at = pl.ds(pl.multiple_of(s * CHUNK, CHUNK), CHUNK)
-            both = dot_bf16(tab_v[at, :], rhs[...])
-            u = both[:, 0:nodes]
-            vel[c, at, :] = u
-            swirl[c, at, :] = both[:, nodes : 2 * nodes]
-            high = u.astype(bf16)
-            low = (u - high.astype(jnp.float32)).astype(bf16)
-            slopes = dot_bf16(jnp.concatenate([high, low, high], axis=1), gmat[...])
-            radial[c, at, :] = slopes[:, 0:nodes]
-            sz = slopes[:, nodes : 2 * nodes]
-            axial[c, at, :] = sz
-            face_send[c, :, at] = dot_bf16(take_edge, sz.astype(bf16), NT)
-            return carry
-
-        lax.fori_loop(0, steps, body, 0)
-        copy = pltpu.make_async_remote_copy(
+        rhs[:, nodes : 2 * nodes] = jnp.where(
+            index % 2 == 0, -wave * after, wave * before
+        ).astype(bf16)
+
+    def slopes_at(c, at, u):
+        high = u.astype(bf16)
+        low = (u - high.astype(jnp.float32)).astype(bf16)
+        slopes = dot_bf16(jnp.concatenate([high, low, high], axis=1), gmat[...])
+        radial[c, at, :] = slopes[:, 0:nodes]
+        sz = slopes[:, nodes : 2 * nodes]
+        axial[c, at, :] = sz
+        face_send[c, :, at] = dot_bf16(take_edge, sz.astype(bf16), NT)
+
+    def face_copy(c):
+        return pltpu.make_async_remote_copy(
             src_ref=face_send.at[c],
             dst_ref=face_recv.at[c],
             send_sem=x_send.at[c],
@@ -443,11 +451,23 @@
             device_id=(me, 1 - mer),
             device_id_type=MESH,
         )
-        copy.start()
-        return copy
-
-    faces = [to_planes(0)]
-
+
+    def to_planes(c):
+        arrived(c)
+        slope_modes(c)
+        rhs[:, 0:nodes] = recv[c]
+
+        def body(at):
+            both = dot_bf16(tab_v[at, :], rhs[...])
+            u = both[:, 0:nodes]
+            vel[c, at, :] = u
+            swirl[c, at, :] = both[:, nodes : 2 * nodes]
+            slopes_at(c, at, u)
+
+        over_planes(body)
+        face_copy(c).start()
+
+    loading[2].wait()
     pltpu.make_async_copy(
         pick_recv.at[pl.ds(0, (n - 1) * 16), :],
         pick_recv.at[pl.ds(0, (n - 1) * 16), :],
@@ -457,73 +477,104 @@
     unit = (iota((128, 128), 0) == iota((128, 128), 1)).astype(jnp.float32).astype(bf16)
     columns = dot_bf16(unit, picked, NT)
     for j in range(jobs):
-        weight = sm[0, 0, j].astype(jnp.float32)
+        weight = sm[j].astype(jnp.float32)
         for i in range(3):
             column = columns[:, i * jobs + j : i * jobs + j + 1]
             scaled[j * 128 : (j + 1) * 128, i * nodes : (i + 1) * nodes] = (
                 column * weight
             ).astype(bf16)
-    loading[2].wait()
-
-    def force(s, carry):
-        at = pl.ds(pl.multiple_of(s * CHUNK, CHUNK), CHUNK)
+    loading[3].wait()
+
+    def force(at):
         lhs = sa_v[:, :, at].reshape(jobs * 128, CHUNK)
         forcing[at, :] = dot_bf16(lhs, scaled[...], TN)
-        return carry
-
-    lax.fori_loop(0, steps, force, 0)
-
-    faces.append(to_planes(1))
-    faces.append(to_planes(2))
-    loading[1].wait()
-
-    def to_modes(i):
-        faces[i].wait()
-
-        def term(s, carry):
-            at = pl.ds(pl.multiple_of(s * CHUNK, CHUNK), CHUNK)
-            ur, ut, uz = vel[0, at, :], vel[1, at, :], vel[2, at, :]
+
+    over_planes(force)
+    loading[4].wait()
+    to_planes(0)
+    to_planes(1)
+
+    for i in range(2):
+        face_copy(i).wait()
+
+    def partial(at):
+        ur, ut = vel[0, at, :], vel[1, at, :]
+        qt = q * ut
+        for i in range(2):
             other = dot_bf16(face_recv[i, :, at].astype(bf16), put_edge, TN)
-            slope_z = axial[i, at, :] + other
-            qt = q * ut
-            value = ur * radial[i, at, :] + uz * slope_z + qt * swirl[i, at, :]
-            if i == 0:
-                value = value - qt * ut
-            if i == 1:
-                value = value + qt * ur
-            total[at, :] = (value + forcing[at, i * nodes : (i + 1) * nodes]).astype(bf16)
-            return carry
-
-        lax.fori_loop(0, steps, term, 0)
-
-        def back(s, carry):
-            at = pl.ds(pl.multiple_of(s * CHUNK, CHUNK), CHUNK)
-            res[i, at, :] = dot_bf16(tabt_v[at, :], total[...]).astype(bf16)
-            return carry
-
-        lax.fori_loop(0, steps, back, 0)
-
-        def send(o, carry):
-            peer = lax.rem(me + o, n)
-            pltpu.make_async_remote_copy(
-                src_ref=res.at[i, pl.ds(pl.multiple_of(peer * local, local), local), :],
-                dst_ref=out.at[i, :, pl.ds(pl.multiple_of(me * nodes, nodes), nodes)],
-                send_sem=b_send.at[i],
-                recv_sem=b_recv.at[i],
-                device_id=(peer, mer),
-                device_id_type=MESH,
+            axial[i, at, :] = axial[i, at, :] + other
+            value = ur * radial[i, at, :] + qt * swirl[i, at, :]
+            value = value - qt * ut if i == 0 else value + qt * ur
+            radial[i, at, :] = value + forcing[at, i * nodes : (i + 1) * nodes]
+
+    over_planes(partial)
+    loading[5].wait()
+
+    arrived(2)
+
+    def first_terms(at):
+        uz = dot_bf16(tab_v[at, :], recv[2])
+        vel[2, at, :] = uz
+        for i in range(2):
+            total[at, i * nodes : (i + 1) * nodes] = (
+                radial[i, at, :] + uz * axial[i, at, :]
+            ).astype(bf16)
+
+    over_planes(first_terms, True)
+
+    peers = CHUNK // local
+    chunk_of, seat = me // peers, lax.rem(me, peers)
+
+    def to_modes(components):
+        count = len(components)
+        for k in (2, 3, 1, 0):
+            chunk = lax.rem(chunk_of + k, steps)
+            at = pl.ds(pl.multiple_of(chunk * CHUNK, CHUNK), CHUNK)
+            back = dot_bf16(tabt_v[at, :], total[:, 0 : count * nodes])
+            for d, i in enumerate(components):
+                res[i, at, :] = back[:, d * nodes : (d + 1) * nodes].astype(bf16)
+            for i in components:
+
+                def send(o, carry):
+                    peer = chunk * peers + lax.rem(seat + o, peers)
+                    pltpu.make_async_remote_copy(
+                        src_ref=res.at[i, pl.ds(pl.multiple_of(peer * local, local), local), :],
+                        dst_ref=out.at[i, :, pl.ds(pl.multiple_of(me * nodes, nodes), nodes)],
+                        send_sem=b_send.at[i],
+                        recv_sem=b_recv.at[i],
+                        device_id=(peer, mer),
+                        device_id_type=MESH,
+                    ).start()
+                    return carry
+
+                lax.fori_loop(1 if k == 0 else 0, peers, send, 0)
+        for i in components:
+            pltpu.make_async_copy(
+                res.at[i, pl.ds(pl.multiple_of(me * local, local), local), :],
+                out.at[i, :, pl.ds(pl.multiple_of(me * nodes, nodes), nodes)],
+                b_recv.at[i],
             ).start()
-            return carry
-
-        lax.fori_loop(1, n, send, 0)
-        pltpu.make_async_copy(
-            res.at[i, pl.ds(pl.multiple_of(me * local, local), local), :],
-            out.at[i, :, pl.ds(pl.multiple_of(me * nodes, nodes), nodes)],
-            b_recv.at[i],
-        ).start()
-
-    for i in range(3):
-        to_modes(i)
+
+    to_modes((0, 1))
+
+    slope_modes(2)
+
+    def own_slopes(at):
+        swirl[2, at, :] = dot_bf16(tab_v[at, :], rhs[:, nodes : 2 * nodes])
+        slopes_at(2, at, vel[2, at, :])
+
+    over_planes(own_slopes)
+    face_copy(2).start()
+    face_copy(2).wait()
+
+    def last_term(at):
+        other = dot_bf16(face_recv[2, :, at].astype(bf16), put_edge, TN)
+        value = vel[0, at, :] * radial[2, at, :] + vel[2, at, :] * (axial[2, at, :] + other)
+        value = value + (q * vel[1, at, :]) * swirl[2, at, :]
+        total[at, 0:nodes] = (value + forcing[at, 2 * nodes : 3 * nodes]).astype(bf16)
+
+    over_planes(last_term)
+    to_modes((2,))
 
     sent = recv.at[0, pl.ds(0, (n - 1) * local), :]
     for c in range(3):
@@ -554,7 +605,7 @@
     nodes = rows * cells
     jobs = spread_tile.shape[2]
     slots = blade_load.shape[1]
-    if local % 16 or lax.axis_size("mer") != 2 or 3 * slots > 16 or jobs != 4:
+    if local % 16 or planes != 4 * CHUNK or CHUNK % local or lax.axis_size("mer") != 2 or 3 * slots > 16 or jobs != 4:
         return on_device(
             velocity_modes,
             geometry,
@@ -574,7 +625,7 @@
     return pl.pallas_call(
         functools.partial(fused_kernel, n, slots),
         out_shape=jax.ShapeDtypeStruct(velocity_modes.shape, bf16),
-        in_specs=[hbm, vmem, vmem, vmem, smem, smem, hbm, vmem, hbm, hbm],
+        in_specs=[hbm, hbm, hbm, vmem, smem, smem, hbm, hbm, hbm, hbm],
         out_specs=hbm,
         scratch_shapes=[
             pltpu.VMEM((3, planes, nodes), bf16),
@@ -584,11 +635,14 @@
             pltpu.VMEM((3, planes, nodes), f32),
             pltpu.VMEM((3, planes, nodes), f32),
             pltpu.VMEM((planes, 3 * nodes), f32),
-            pltpu.VMEM((planes, nodes), bf16),
+            pltpu.VMEM((planes, 2 * nodes), bf16),
             pltpu.VMEM((3, planes, nodes), bf16),
             pltpu.VMEM((planes, planes), bf16),
             pltpu.VMEM((planes, planes), bf16),
             pltpu.VMEM((jobs, TILE, planes), bf16),
+            pltpu.VMEM((jobs, TILE, nodes), bf16),
+            pltpu.VMEM(geometry.shape, f32),
+            pltpu.VMEM(derivative.shape, f32),
             pltpu.VMEM((jobs * TILE, 3 * nodes), bf16),
             pltpu.VMEM((3 * nodes, 2 * nodes), bf16),
             pltpu.VMEM((16, blade_load.shape[3]), f32),
@@ -606,10 +660,10 @@
             dma((2,)),
             dma((3,)),
             dma((3,)),
-            dma((3,)),
+            dma((6,)),
         ],
         compiler_params=pltpu.CompilerParams(
-            collective_id=0, has_side_effects=True, vmem_limit_bytes=48 * 1024 * 1024
+            collective_id=0, has_side_effects=True, vmem_limit_bytes=60 * 1024 * 1024
         ),
     )(
         velocity_modes,

time: 62.9 us -> 54.2 us (0.86)
  the two profiles are of different devices: /device:TPU:0 before, /device:TPU:17 now
where the time goes in v1:
time: 54.2 us; the launch traced here: 54 us
  Pallas kernels  51.9 us (96%)
  local copies, waits for them, and re-layouts  2.09 us (4%)
    pallas_call x1, Pallas kernels, on_device_fused(): pl.pallas_call(functools.partial(fused_kernel, n, slots), out_shape=jax.S...  51.9 us
    unnamed x1, local copies, waits for them, and re-layouts  2.09 us

profile of v1, /device:TPU:17, one launch (start us, length us, event | category | flops | bytes accessed | tf_op | source)
XLA Modules:
  0.0 54.0 jit_solution(18177273144643215980)
XLA Ops:
  0.0 51.9 %shard_map.100 = bf16[3,64,2048]{2,1,0:T(8,128)(2,1)} custom-call(bf16[3,64,2048]{2,1,0:T(8,128)(2,1)} %vm.1, f32[3,8,16]{2,1,0:T(8,128)} %geo_in.1, f32[2,8,8]{2,1,0:T(8,128)} %der_in.1, bf16[1,3,3,1024]{3,2,1,0:T(4,128)(2,1)} %loads.1, s32[36]{0:T(128)} %owner.1, s32[1,1,4]{2,1,0:T(1,128)} %tile.1, bf16[1,1,4,128,1024]{4,3,2,1,0:T(8,128)(2,1)} %sa.1, ...), custom_call_target="tpu_custom_call" | custom-call | tf_op jit(solution)/shard_map/pallas_call | solution.py:625
  51.9 2.1 %copy.12 = bf16[3,64,2048]{2,1,0:T(8,128)(2,1)} copy(bf16[3,64,2048]{2,1,0:T(8,128)(2,1)} %shard_map.100) | data formatting | bytes 1572864

commit v2 on v1

--- a/solution.py
+++ b/solution.py
@@ -225,9 +225,9 @@
     vm,
     geo_in,
     der_in,
-    loads,
-    owner,
-    tile,
+    loads_in,
+    owner_in,
+    tile_in,
     sa,
     sm_in,
     table,
@@ -248,6 +248,9 @@
     sm,
     geo,
     der,
+    loads,
+    owner,
+    tile,
     scaled,
     gmat,
     load_rows,
@@ -277,17 +280,11 @@
     steps = planes // CHUNK
     bf16 = jnp.bfloat16
 
-    barrier = pltpu.get_barrier_semaphore()
-
-    def greet(o, carry):
-        pl.semaphore_signal(
-            barrier, inc=1, device_id=(lax.rem(me + o, n), mer), device_id_type=MESH
-        )
-        return carry
-
-    lax.fori_loop(1, n, greet, 0)
-    pl.semaphore_signal(barrier, inc=1, device_id=(me, 1 - mer), device_id_type=MESH)
-
+    small = [
+        pltpu.make_async_copy(owner_in, owner, local_sem.at[6]),
+        pltpu.make_async_copy(tile_in, tile, local_sem.at[7]),
+        pltpu.make_async_copy(loads_in, loads, local_sem.at[8]),
+    ]
     loading = [
         pltpu.make_async_copy(geo_in, geo, local_sem.at[0]),
         pltpu.make_async_copy(der_in, der, local_sem.at[1]),
@@ -296,24 +293,39 @@
         pltpu.make_async_copy(table, tab_v, local_sem.at[4]),
         pltpu.make_async_copy(table_t, tabt_v, local_sem.at[5]),
     ]
-
-    row8 = iota((8, 128), 0) % jobs
-    codes = jnp.zeros((8, 128), jnp.int32)
+    for copy in small + loading[:5]:
+        copy.start()
+
+    barrier = pltpu.get_barrier_semaphore()
+
+    def greet(o, carry):
+        pl.semaphore_signal(
+            barrier, inc=1, device_id=(lax.rem(me + o, n), mer), device_id_type=MESH
+        )
+        return carry
+
+    lax.fori_loop(1, n, greet, 0)
+    pl.semaphore_signal(barrier, inc=1, device_id=(me, 1 - mer), device_id_type=MESH)
+
+    small[0].wait()
+    small[1].wait()
+    job = iota((1, 128), 1) % jobs
+    codes = jnp.zeros((1, 128), jnp.int32)
     tiles_per_blade = loads.shape[3] // 128
     for j in range(jobs):
         t = tile[0, 0, j]
         code = owner[t // tiles_per_blade] * tiles_per_blade + lax.rem(t, tiles_per_blade)
-        codes = jnp.where(row8 == j, code, codes)
-    ids_send[...] = codes
-    ids_recv[pl.ds(pl.multiple_of(me * 8, 8), 8), :] = codes
+        codes = jnp.where(job == j, code, codes)
+    ids_send[0] = codes
+    ids_recv[me] = codes
 
     pl.semaphore_wait(barrier, n)
 
     def send_ids(o, carry):
         peer = lax.rem(me + o, n)
         pltpu.make_async_remote_copy(
-            src_ref=ids_send,
-            dst_ref=ids_recv.at[pl.ds(pl.multiple_of(me * 8, 8), 8), :],
+            src_ref=ids_send.at[0],
+            dst_ref=ids_recv.at[me],
             send_sem=small_send.at[0],
             recv_sem=small_recv.at[0],
             device_id=(peer, mer),
@@ -344,20 +356,47 @@
         ).start()
 
     send_forward(0)
-    for copy in loading:
-        copy.start()
-
+    send_forward(1)
+
+    loading[0].wait()
+    loading[1].wait()
+    edge = (1 - mer) * (cells - 1)
+    q = geometry_row(geo[0], cells, nodes)
+    grad_r, grad_z = slope_matrices(
+        der,
+        geometry_row(geo[1], cells, nodes),
+        geometry_row(geo[2], cells, nodes),
+        rows,
+        cells,
+        edge,
+    )
+    for side, grad in ((0, grad_r), (1, grad_z)):
+        high = grad.astype(bf16)
+        low = (grad - high.astype(jnp.float32)).astype(bf16)
+        at = slice(side * nodes, (side + 1) * nodes)
+        gmat[0:nodes, at] = high
+        gmat[nodes : 2 * nodes, at] = high
+        gmat[2 * nodes : 3 * nodes, at] = low
+    lane = iota((rows, nodes), 1)
+    on_edge = (lane // cells == iota((rows, nodes), 0)) & (lane % cells == edge)
+    take_edge = jnp.where(on_edge, 2.0, 0.0).astype(bf16)
+    put_edge = jnp.where(on_edge, 0.5, 0.0).astype(bf16)
+
+    small[2].wait()
     load_rows[...] = jnp.zeros(load_rows.shape, jnp.float32)
     for s in range(slots):
         load_rows[3 * s : 3 * s + 3, :] = loads[0, s].astype(jnp.float32)
 
     pltpu.make_async_copy(
-        ids_recv.at[pl.ds(0, (n - 1) * 8), :],
-        ids_recv.at[pl.ds(0, (n - 1) * 8), :],
+        ids_recv.at[pl.ds(0, n - 1)],
+        ids_recv.at[pl.ds(0, n - 1)],
         small_recv.at[0],
     ).wait()
-    asked = ids_recv[...].reshape(n, 8, 128)
-    asked = jnp.concatenate([asked, asked], axis=1).reshape(n * 16, 128)
+    asked = jnp.broadcast_to(ids_recv[...], (n, 16, 128)).reshape(n * 16, 128)
+    for_row = iota((n * 16, 128), 1) % jobs == iota((n * 16, 128), 0) % jobs
+    asked = jnp.where(for_row, asked.astype(jnp.float32), 0.0)
+    asked = jnp.max(asked, axis=1, keepdims=True).astype(jnp.int32)
+    asked = jnp.broadcast_to(asked, (n * 16, 128))
     part = (iota((n * 16, 128), 0) % 16) // jobs
     slot = asked // tiles_per_blade - me * slots
     wanted = slot * 3 + part
@@ -386,32 +425,8 @@
         return carry
 
     lax.fori_loop(1, n, send_picks, 0)
-    send_forward(1)
     send_forward(2)
-
-    loading[0].wait()
-    loading[1].wait()
-    edge = (1 - mer) * (cells - 1)
-    q = geometry_row(geo[0], cells, nodes)
-    grad_r, grad_z = slope_matrices(
-        der,
-        geometry_row(geo[1], cells, nodes),
-        geometry_row(geo[2], cells, nodes),
-        rows,
-        cells,
-        edge,
-    )
-    for side, grad in ((0, grad_r), (1, grad_z)):
-        high = grad.astype(bf16)
-        low = (grad - high.astype(jnp.float32)).astype(bf16)
-        at = slice(side * nodes, (side + 1) * nodes)
-        gmat[0:nodes, at] = high
-        gmat[nodes : 2 * nodes, at] = high
-        gmat[2 * nodes : 3 * nodes, at] = low
-    lane = iota((rows, nodes), 1)
-    on_edge = (lane // cells == iota((rows, nodes), 0)) & (lane % cells == edge)
-    take_edge = jnp.where(on_edge, 2.0, 0.0).astype(bf16)
-    put_edge = jnp.where(on_edge, 0.5, 0.0).astype(bf16)
+    loading[5].start()
 
     def over_planes(body, unroll=False):
         def step(s, carry):
@@ -466,6 +481,10 @@
 
         over_planes(body)
         face_copy(c).start()
+
+    loading[4].wait()
+    to_planes(0)
+    to_planes(1)
 
     loading[2].wait()
     pltpu.make_async_copy(
@@ -490,9 +509,6 @@
         forcing[at, :] = dot_bf16(lhs, scaled[...], TN)
 
     over_planes(force)
-    loading[4].wait()
-    to_planes(0)
-    to_planes(1)
 
     for i in range(2):
         face_copy(i).wait()
@@ -526,34 +542,33 @@
     chunk_of, seat = me // peers, lax.rem(me, peers)
 
     def to_modes(components):
-        count = len(components)
+        count, first = len(components), components[0]
+        these = pl.ds(first, count)
         for k in (2, 3, 1, 0):
             chunk = lax.rem(chunk_of + k, steps)
             at = pl.ds(pl.multiple_of(chunk * CHUNK, CHUNK), CHUNK)
             back = dot_bf16(tabt_v[at, :], total[:, 0 : count * nodes])
             for d, i in enumerate(components):
                 res[i, at, :] = back[:, d * nodes : (d + 1) * nodes].astype(bf16)
-            for i in components:
-
-                def send(o, carry):
-                    peer = chunk * peers + lax.rem(seat + o, peers)
-                    pltpu.make_async_remote_copy(
-                        src_ref=res.at[i, pl.ds(pl.multiple_of(peer * local, local), local), :],
-                        dst_ref=out.at[i, :, pl.ds(pl.multiple_of(me * nodes, nodes), nodes)],
-                        send_sem=b_send.at[i],
-                        recv_sem=b_recv.at[i],
-                        device_id=(peer, mer),
-                        device_id_type=MESH,
-                    ).start()
-                    return carry
-
-                lax.fori_loop(1 if k == 0 else 0, peers, send, 0)
-        for i in components:
-            pltpu.make_async_copy(
-                res.at[i, pl.ds(pl.multiple_of(me * local, local), local), :],
-                out.at[i, :, pl.ds(pl.multiple_of(me * nodes, nodes), nodes)],
-                b_recv.at[i],
-            ).start()
+
+            def send(o, carry):
+                peer = chunk * peers + lax.rem(seat + o, peers)
+                pltpu.make_async_remote_copy(
+                    src_ref=res.at[these, pl.ds(pl.multiple_of(peer * local, local), local), :],
+                    dst_ref=out.at[these, :, pl.ds(pl.multiple_of(me * nodes, nodes), nodes)],
+                    send_sem=b_send.at[first],
+                    recv_sem=b_recv.at[first],
+                    device_id=(peer, mer),
+                    device_id_type=MESH,
+                ).start()
+                return carry
+
+            lax.fori_loop(1 if k == 0 else 0, peers, send, 0)
+        pltpu.make_async_copy(
+            res.at[these, pl.ds(pl.multiple_of(me * local, local), local), :],
+            out.at[these, :, pl.ds(pl.multiple_of(me * nodes, nodes), nodes)],
+            b_recv.at[first],
+        ).start()
 
     to_modes((0, 1))
 
@@ -579,13 +594,15 @@
     sent = recv.at[0, pl.ds(0, (n - 1) * local), :]
     for c in range(3):
         pltpu.make_async_copy(sent, sent, f_send.at[c]).wait()
-        pltpu.make_async_copy(sent, sent, b_send.at[c]).wait()
-    sent = ids_recv.at[pl.ds(0, (n - 1) * 8), :]
+    sent = ids_recv.at[pl.ds(0, n - 1)]
     pltpu.make_async_copy(sent, sent, small_send.at[0]).wait()
     sent = pick_recv.at[pl.ds(0, (n - 1) * 16), :]
     pltpu.make_async_copy(sent, sent, small_send.at[1]).wait()
-    for c in range(3):
-        pltpu.make_async_copy(out.at[c], out.at[c], b_recv.at[c]).wait()
+    for first, count in ((0, 2), (2, 1)):
+        sent = recv.at[pl.ds(first, count), pl.ds(0, (n - 1) * local), :]
+        pltpu.make_async_copy(sent, sent, b_send.at[first]).wait()
+        landed = out.at[pl.ds(first, count)]
+        pltpu.make_async_copy(landed, landed, b_recv.at[first]).wait()
 
 
 def on_device_fused(
@@ -618,15 +635,13 @@
         )
     table = host_table(planes)
     bf16, f32 = jnp.bfloat16, jnp.float32
-    vmem = pl.BlockSpec(memory_space=pltpu.VMEM)
-    smem = pl.BlockSpec(memory_space=pltpu.SMEM)
-    hbm = pl.BlockSpec(memory_space=pl.ANY)
+    hbm = pl.BlockSpec(memory_space=pltpu.HBM)
     dma = pltpu.SemaphoreType.DMA
     return pl.pallas_call(
         functools.partial(fused_kernel, n, slots),
         out_shape=jax.ShapeDtypeStruct(velocity_modes.shape, bf16),
-        in_specs=[hbm, hbm, hbm, vmem, smem, smem, hbm, hbm, hbm, hbm],
-        out_specs=hbm,
+        in_specs=[hbm] * 10,
+        out_specs=pl.BlockSpec(memory_space=pl.ANY),
         scratch_shapes=[
             pltpu.VMEM((3, planes, nodes), bf16),
             pltpu.VMEM((planes, 2 * nodes), bf16),
@@ -643,11 +658,14 @@
             pltpu.VMEM((jobs, TILE, nodes), bf16),
             pltpu.VMEM(geometry.shape, f32),
             pltpu.VMEM(derivative.shape, f32),
+            pltpu.VMEM(blade_load.shape, bf16),
+            pltpu.SMEM(blade_owner.shape, jnp.int32),
+            pltpu.SMEM(spread_tile.shape, jnp.int32),
             pltpu.VMEM((jobs * TILE, 3 * nodes), bf16),
             pltpu.VMEM((3 * nodes, 2 * nodes), bf16),
             pltpu.VMEM((16, blade_load.shape[3]), f32),
-            pltpu.VMEM((8, 128), jnp.int32),
-            pltpu.VMEM((n * 8, 128), jnp.int32),
+            pltpu.VMEM((1, 1, 128), jnp.int32),
+            pltpu.VMEM((n, 1, 128), jnp.int32),
             pltpu.VMEM((n * 16, 128), bf16),
             pltpu.VMEM((n * 16, 128), bf16),
             pltpu.VMEM((3, rows, planes), f32),
@@ -660,7 +678,7 @@
             dma((2,)),
             dma((3,)),
             dma((3,)),
-            dma((6,)),
+            dma((9,)),
         ],
         compiler_params=pltpu.CompilerParams(
             collective_id=0, has_side_effects=True, vmem_limit_bytes=60 * 1024 * 1024

time: 54.2 us -> 50 us (0.923)
  the two profiles are of different devices: /device:TPU:17 before, /device:TPU:0 now
where the time goes in v2:
time: 50 us; the launch traced here: 49.9 us
  Pallas kernels  47.8 us (96%)
  local copies, waits for them, and re-layouts  2.09 us (4%)
    pallas_call x1, Pallas kernels, on_device_fused(): pl.pallas_call(functools.partial(fused_kernel, n, slots), out_shape=jax.S...  47.8 us
    unnamed x1, local copies, waits for them, and re-layouts  2.09 us

profile of v2, /device:TPU:0, one launch (start us, length us, event | category | flops | bytes accessed | tf_op | source)
XLA Modules:
  0.0 49.9 jit_solution(4847035373350701490)
XLA Ops:
  0.0 47.8 %shard_map.100 = bf16[3,64,2048]{2,1,0:T(8,128)(2,1)} custom-call(bf16[3,64,2048]{2,1,0:T(8,128)(2,1)} %vm.1, f32[3,8,16]{2,1,0:T(8,128)} %geo_in.1, f32[2,8,8]{2,1,0:T(8,128)} %der_in.1, bf16[1,3,3,1024]{3,2,1,0:T(4,128)(2,1)} %loads_in.1, s32[36]{0:T(128)} %owner_in.1, s32[1,1,4]{2,1,0:T(1,128)} %tile_in.1, bf16[1,1,4,128,1024]{4,3,2,1,0:T(8,128)(2,1)} %sa.1, ...), custom_call_target="tpu_custom_call" | custom-call | tf_op jit(solution)/shard_map/pallas_call | solution.py:640
  47.8 2.1 %copy.12 = bf16[3,64,2048]{2,1,0:T(8,128)(2,1)} copy(bf16[3,64,2048]{2,1,0:T(8,128)(2,1)} %shard_map.100) | data formatting | bytes 1572864

commit v3 on v2

--- a/solution.py
+++ b/solution.py
@@ -428,7 +428,7 @@
     send_forward(2)
     loading[5].start()
 
-    def over_planes(body, unroll=False):
+    def over_planes(body, unroll=True):
         def step(s, carry):
             body(pl.ds(pl.multiple_of(s * CHUNK, CHUNK), CHUNK))
             return carry
@@ -510,15 +510,10 @@
 
     over_planes(force)
 
-    for i in range(2):
-        face_copy(i).wait()
-
     def partial(at):
         ur, ut = vel[0, at, :], vel[1, at, :]
         qt = q * ut
         for i in range(2):
-            other = dot_bf16(face_recv[i, :, at].astype(bf16), put_edge, TN)
-            axial[i, at, :] = axial[i, at, :] + other
             value = ur * radial[i, at, :] + qt * swirl[i, at, :]
             value = value - qt * ut if i == 0 else value + qt * ur
             radial[i, at, :] = value + forcing[at, i * nodes : (i + 1) * nodes]
@@ -526,6 +521,15 @@
     over_planes(partial)
     loading[5].wait()
 
+    for i in range(2):
+        face_copy(i).wait()
+
+    def add_faces(at):
+        for i in range(2):
+            other = dot_bf16(face_recv[i, :, at].astype(bf16), put_edge, TN)
+            axial[i, at, :] = axial[i, at, :] + other
+
+    over_planes(add_faces)
     arrived(2)
 
     def first_terms(at):

time: 50 us -> 48.7 us (0.974)
  Pallas kernels: 47.8 us -> 46.5 us
    pallas_call x1, Pallas kernels: 47.8 us -> 46.5 us  [on_device_fused(): pl.pallas_call(functools.partial(fused_kernel, n, slots), out_shape=jax.S...]
where the time goes in v3:
time: 48.7 us; the launch traced here: 48.6 us
  Pallas kernels  46.5 us (95%)
  local copies, waits for them, and re-layouts  2.09 us (4%)
    pallas_call x1, Pallas kernels, on_device_fused(): pl.pallas_call(functools.partial(fused_kernel, n, slots), out_shape=jax.S...  46.5 us
    unnamed x1, local copies, waits for them, and re-layouts  2.09 us

profile of v3, /device:TPU:0, one launch (start us, length us, event | category | flops | bytes accessed | tf_op | source)
XLA Modules:
  0.0 48.6 jit_solution(10432407575299169286)
XLA Ops:
  0.0 46.5 %shard_map.100 = bf16[3,64,2048]{2,1,0:T(8,128)(2,1)} custom-call(bf16[3,64,2048]{2,1,0:T(8,128)(2,1)} %vm.1, f32[3,8,16]{2,1,0:T(8,128)} %geo_in.1, f32[2,8,8]{2,1,0:T(8,128)} %der_in.1, bf16[1,3,3,1024]{3,2,1,0:T(4,128)(2,1)} %loads_in.1, s32[36]{0:T(128)} %owner_in.1, s32[1,1,4]{2,1,0:T(1,128)} %tile_in.1, bf16[1,1,4,128,1024]{4,3,2,1,0:T(8,128)(2,1)} %sa.1, ...), custom_call_target="tpu_custom_call" | custom-call | tf_op jit(solution)/shard_map/pallas_call | solution.py:644
  46.5 2.1 %copy.12 = bf16[3,64,2048]{2,1,0:T(8,128)(2,1)} copy(bf16[3,64,2048]{2,1,0:T(8,128)(2,1)} %shard_map.100) | data formatting | bytes 1572864
